TPU v7x, 32 devices: a whole 2x2x4 slice. The times are simulated.
32 devices in a mesh: space: 16 (over z, y, x), batch: 2 (over core).
Axes of the slice: x: 2, y: 2, z: 4, core: 2. Of those that a mesh axis runs over, the one named last changes fastest.
Arguments:
- features: bfloat16 [2, 8192, 128], P('batch', 'space'), may hold values from -6 to 6
- weights: bfloat16 [27, 128, 128], replicated, may hold values from -0.109375 to 0.109375
- kernel_map: int32 [2, 27, 8192], P('batch', None, 'space'), may hold values from 0 to 768, as said below
- send_rows: int32 [2, 2, 2048], P('batch', None, 'space'), may hold values from 0 to 511, as said below
- counts: int32 [2, 16], P('batch', 'space'), may hold values from 64 to 512, as said below
- cotangent: bfloat16 [2, 8192, 128], P('batch', 'space'), may hold values from -6 to 6
Outputs:
- output: bfloat16 [2, 8192, 128], P('batch', 'space')
- grad_features: bfloat16 [2, 8192, 128], P('batch', 'space')
- grad_weights: float32 [27, 128, 128], replicated
Inputs may be any that keep to these rules, and one draw needn't show every extreme that they name: `kernel_map`: values below 512 are active slots of the same block (below its count); 512 to 639 are rows received from the lower block, the next 128 rows from the upper block, 768 is the zero row. The first block never reads the lower rows, the last never the upper ones. The middle offset reads each active slot itself; inactive slots read only the zero row. `send_rows`: every entry is an active slot of the sending block. `counts`: each scene tile has a block with all 512 slots active and a block with exactly 64; every block has at least 64.
All inputs are finite; a program needn't handle non-finite values.
Results may differ from a plain program's by a relative error of at most 0.001.
Values may be sent and summed in bfloat16 or wider, within the bound.
A program may use at most 64 MiB of HBM per device.

v0:
```python
import jax
import jax.numpy as jnp
from jax import lax
from jax.sharding import PartitionSpec as P


def with_halo(shard, sides, width):
    for axis, dim in sides:
        size, length = (lax.axis_size(axis), shard.shape[dim])
        up = [(i, (i + 1) % size) for i in range(size - 1)]
        down = [(j, i) for i, j in up]
        last = lax.slice_in_dim(shard, length - width, length, axis=dim)
        first = lax.slice_in_dim(shard, 0, width, axis=dim)
        before = lax.ppermute(last, axis, up)
        after = lax.ppermute(first, axis, down)
        shard = jnp.concatenate([before, shard, after], axis=dim)
    return shard


def per_device(features, weights, kernel_map, send_rows, counts, cotangent):
    slots = features.shape[1]
    channels = features.shape[2]
    offsets = weights.shape[0]
    alive = (lax.iota(jnp.int32, slots) < counts[0, 0])[:, None]
    live = jnp.where(alive, features[0], jnp.zeros((), jnp.bfloat16))
    zero_row = jnp.zeros((1, channels), jnp.bfloat16)
    padded = jnp.concatenate([live, zero_row], 0)
    send_lists = send_rows[0]
    halo_width = send_lists.shape[1]
    outgoing = padded[send_lists]
    beside_all = with_halo(outgoing, (("space", 0),), 1)
    extended = jnp.concatenate([live, beside_all[0], beside_all[3], zero_row], 0)
    offset_map = kernel_map[0]

    def forward_step(running, pair):
        source, weight = pair
        return (
            running + jnp.dot(extended[source], weight, preferred_element_type=jnp.float32),
            None,
        )

    result, unused = lax.scan(
        forward_step, jnp.zeros((slots, channels), jnp.float32), (offset_map, weights)
    )
    output = jnp.where(alive, result, jnp.zeros((), jnp.float32)).astype(jnp.bfloat16)
    grad_rows = jnp.where(alive, cotangent[0], jnp.zeros((), jnp.bfloat16))

    def backward_step(accum_grad, pair):
        source, weight = pair
        gathered = extended[source]
        weight_part = lax.dot_general(
            gathered, grad_rows, (((0,), (0,)), ((), ())), preferred_element_type=jnp.float32
        )
        contrib = jnp.dot(grad_rows, weight.T, preferred_element_type=jnp.float32)
        return (accum_grad.at[source].add(contrib), weight_part)

    ext_length = slots + 2 * halo_width + 1
    ext_grad, weight_parts = lax.scan(
        backward_step, jnp.zeros((ext_length, channels), jnp.float32), (offset_map, weights)
    )
    halo_grads = jnp.stack(
        [
            ext_grad[slots : slots + halo_width],
            ext_grad[slots + halo_width : slots + 2 * halo_width],
        ],
        0,
    )
    returned = with_halo(halo_grads, (("space", 0),), 1)
    local_grads = jnp.concatenate([ext_grad[:slots], jnp.zeros((1, channels), jnp.float32)], 0)
    local_grads = local_grads.at[send_lists[1]].add(returned[3]).at[send_lists[0]].add(returned[0])
    grad_features = jnp.where(alive, local_grads[:slots], jnp.zeros((), jnp.float32)).astype(
        jnp.bfloat16
    )
    flat_parts = weight_parts.reshape(offsets * channels, channels)
    summed = lax.psum(flat_parts, ("space", "batch"))
    total_rows = slots * lax.axis_size("space") * lax.axis_size("batch")
    grad_weights = (summed * total_rows ** (-0.5)).reshape(offsets, channels, channels)
    return (output[None], grad_features[None], grad_weights)


def solution(mesh):
    in_specs = (
        P("batch", "space", None),
        P(),
        P("batch", None, "space"),
        P("batch", None, "space"),
        P("batch", "space"),
        P("batch", "space", None),
    )
    out_specs = (P("batch", "space", None), P("batch", "space", None), P())
    return jax.shard_map(
        per_device, mesh=mesh, in_specs=in_specs, out_specs=out_specs, check_vma=False
    )
```

profile of v0, /device:TPU:0, one launch (start us, length us, event | category | flops | bytes accessed | tf_op | source)
XLA Modules:
  0.0 372.2 jit_solution(17893494904741254546)
XLA Ops:
  10.5 4.8 %collective-permute-start = (bf16[1,128,128]{2,1,0:T(8,128)(2,1)S(1)}, bf16[1,128,128]{2,1,0:T(8,128)(2,1)S(1)}, u32[]{:S(2)}, u32[]{:S(2)}) collective-permute-start(bf16[1,128,128]{2,1,0:T(8,128)(2,1)S(1)} %get-tuple-element.115), channel_id=1, source_target_pairs={{0,2},{2,4},{4,6},{6,8},{8,10},{10,12},{12,14},{14,16},{16,18},{18... | collective-permute-start | bytes 98312 | tf_op jit(solution)/shard_map/ppermute | solution.py:14
  18.3 2.9 collective-permute-done.1
  21.4 200.1 %while.23 = (s32[]{:T(128)}, f32[769,128]{1,0:T(8,128)S(1)}, f32[27,128,128]{2,1,0:T(8,128)}, s32[27,512]{1,0:T(8,128)S(1)}, bf16[27,128,128]{2,1,0:T(8,128)(2,1...) while((s32[]{:T(128)}, f32[769,128]{1,0:T(8,128)S(1)}, ...), condition=%wide.region_4.5_spmd, body=%wide.region_2.4_spmd.sunk | while | flops 33622528 | bytes 2341977 | solution.py:58
  21.5 1.3 gather_fusion
  24.8 4.1 %scatter_fusion = f32[769,128]{1,0:T(8,128)S(1)} fusion(f32[769,128]{1,0:T(8,128)S(1)} %get-tuple-element.206, s32[512]{0:T(512)S(1)} %bitcast.93, f32[512,128]{1,0:T(8,128)S(1)} %copy.15), kind=kCustom, calls=%fused_computation.3.clone.1 | custom fusion | flops 65536 | bytes 788480 | tf_op jit(solution)/shard_map/while/body/eval_jaxpr/scatter-add | solution.py:55
  28.9 1.3 gather_fusion
  32.2 4.1 %scatter_fusion = f32[769,128]{1,0:T(8,128)S(1)} fusion(f32[769,128]{1,0:T(8,128)S(1)} %get-tuple-element.206, s32[512]{0:T(512)S(1)} %bitcast.93, f32[512,128]{1,0:T(8,128)S(1)} %copy.15), kind=kCustom, calls=%fused_computation.3.clone.1 | custom fusion | flops 65536 | bytes 788480 | tf_op jit(solution)/shard_map/while/body/eval_jaxpr/scatter-add | solution.py:55
  36.3 1.3 gather_fusion
  39.6 4.1 %scatter_fusion = f32[769,128]{1,0:T(8,128)S(1)} fusion(f32[769,128]{1,0:T(8,128)S(1)} %get-tuple-element.206, s32[512]{0:T(512)S(1)} %bitcast.93, f32[512,128]{1,0:T(8,128)S(1)} %copy.15), kind=kCustom, calls=%fused_computation.3.clone.1 | custom fusion | flops 65536 | bytes 788480 | tf_op jit(solution)/shard_map/while/body/eval_jaxpr/scatter-add | solution.py:55
  43.7 1.3 gather_fusion
  47.0 4.1 %scatter_fusion = f32[769,128]{1,0:T(8,128)S(1)} fusion(f32[769,128]{1,0:T(8,128)S(1)} %get-tuple-element.206, s32[512]{0:T(512)S(1)} %bitcast.93, f32[512,128]{1,0:T(8,128)S(1)} %copy.15), kind=kCustom, calls=%fused_computation.3.clone.1 | custom fusion | flops 65536 | bytes 788480 | tf_op jit(solution)/shard_map/while/body/eval_jaxpr/scatter-add | solution.py:55
  51.1 1.3 gather_fusion
  54.4 4.1 %scatter_fusion = f32[769,128]{1,0:T(8,128)S(1)} fusion(f32[769,128]{1,0:T(8,128)S(1)} %get-tuple-element.206, s32[512]{0:T(512)S(1)} %bitcast.93, f32[512,128]{1,0:T(8,128)S(1)} %copy.15), kind=kCustom, calls=%fused_computation.3.clone.1 | custom fusion | flops 65536 | bytes 788480 | tf_op jit(solution)/shard_map/while/body/eval_jaxpr/scatter-add | solution.py:55
  58.5 1.3 gather_fusion
  61.8 4.1 %scatter_fusion = f32[769,128]{1,0:T(8,128)S(1)} fusion(f32[769,128]{1,0:T(8,128)S(1)} %get-tuple-element.206, s32[512]{0:T(512)S(1)} %bitcast.93, f32[512,128]{1,0:T(8,128)S(1)} %copy.15), kind=kCustom, calls=%fused_computation.3.clone.1 | custom fusion | flops 65536 | bytes 788480 | tf_op jit(solution)/shard_map/while/body/eval_jaxpr/scatter-add | solution.py:55
  65.9 1.3 gather_fusion
  69.2 4.1 %scatter_fusion = f32[769,128]{1,0:T(8,128)S(1)} fusion(f32[769,128]{1,0:T(8,128)S(1)} %get-tuple-element.206, s32[512]{0:T(512)S(1)} %bitcast.93, f32[512,128]{1,0:T(8,128)S(1)} %copy.15), kind=kCustom, calls=%fused_computation.3.clone.1 | custom fusion | flops 65536 | bytes 788480 | tf_op jit(solution)/shard_map/while/body/eval_jaxpr/scatter-add | solution.py:55
  73.3 1.3 gather_fusion
  76.6 4.1 %scatter_fusion = f32[769,128]{1,0:T(8,128)S(1)} fusion(f32[769,128]{1,0:T(8,128)S(1)} %get-tuple-element.206, s32[512]{0:T(512)S(1)} %bitcast.93, f32[512,128]{1,0:T(8,128)S(1)} %copy.15), kind=kCustom, calls=%fused_computation.3.clone.1 | custom fusion | flops 65536 | bytes 788480 | tf_op jit(solution)/shard_map/while/body/eval_jaxpr/scatter-add | solution.py:55
  80.7 1.3 gather_fusion
  84.0 4.1 %scatter_fusion = f32[769,128]{1,0:T(8,128)S(1)} fusion(f32[769,128]{1,0:T(8,128)S(1)} %get-tuple-element.206, s32[512]{0:T(512)S(1)} %bitcast.93, f32[512,128]{1,0:T(8,128)S(1)} %copy.15), kind=kCustom, calls=%fused_computation.3.clone.1 | custom fusion | flops 65536 | bytes 788480 | tf_op jit(solution)/shard_map/while/body/eval_jaxpr/scatter-add | solution.py:55
  88.2 1.3 gather_fusion
  91.4 4.1 %scatter_fusion = f32[769,128]{1,0:T(8,128)S(1)} fusion(f32[769,128]{1,0:T(8,128)S(1)} %get-tuple-element.206, s32[512]{0:T(512)S(1)} %bitcast.93, f32[512,128]{1,0:T(8,128)S(1)} %copy.15), kind=kCustom, calls=%fused_computation.3.clone.1 | custom fusion | flops 65536 | bytes 788480 | tf_op jit(solution)/shard_map/while/body/eval_jaxpr/scatter-add | solution.py:55
  95.6 1.3 gather_fusion
  98.9 4.1 %scatter_fusion = f32[769,128]{1,0:T(8,128)S(1)} fusion(f32[769,128]{1,0:T(8,128)S(1)} %get-tuple-element.206, s32[512]{0:T(512)S(1)} %bitcast.93, f32[512,128]{1,0:T(8,128)S(1)} %copy.15), kind=kCustom, calls=%fused_computation.3.clone.1 | custom fusion | flops 65536 | bytes 788480 | tf_op jit(solution)/shard_map/while/body/eval_jaxpr/scatter-add | solution.py:55
  103.0 1.3 gather_fusion
  106.3 4.1 %scatter_fusion = f32[769,128]{1,0:T(8,128)S(1)} fusion(f32[769,128]{1,0:T(8,128)S(1)} %get-tuple-element.206, s32[512]{0:T(512)S(1)} %bitcast.93, f32[512,128]{1,0:T(8,128)S(1)} %copy.15), kind=kCustom, calls=%fused_computation.3.clone.1 | custom fusion | flops 65536 | bytes 788480 | tf_op jit(solution)/shard_map/while/body/eval_jaxpr/scatter-add | solution.py:55
  110.4 1.3 gather_fusion
  113.7 4.1 %scatter_fusion = f32[769,128]{1,0:T(8,128)S(1)} fusion(f32[769,128]{1,0:T(8,128)S(1)} %get-tuple-element.206, s32[512]{0:T(512)S(1)} %bitcast.93, f32[512,128]{1,0:T(8,128)S(1)} %copy.15), kind=kCustom, calls=%fused_computation.3.clone.1 | custom fusion | flops 65536 | bytes 788480 | tf_op jit(solution)/shard_map/while/body/eval_jaxpr/scatter-add | solution.py:55
  117.8 1.3 gather_fusion
  121.1 4.1 %scatter_fusion = f32[769,128]{1,0:T(8,128)S(1)} fusion(f32[769,128]{1,0:T(8,128)S(1)} %get-tuple-element.206, s32[512]{0:T(512)S(1)} %bitcast.93, f32[512,128]{1,0:T(8,128)S(1)} %copy.15), kind=kCustom, calls=%fused_computation.3.clone.1 | custom fusion | flops 65536 | bytes 788480 | tf_op jit(solution)/shard_map/while/body/eval_jaxpr/scatter-add | solution.py:55
  125.2 1.3 gather_fusion
  128.5 4.1 %scatter_fusion = f32[769,128]{1,0:T(8,128)S(1)} fusion(f32[769,128]{1,0:T(8,128)S(1)} %get-tuple-element.206, s32[512]{0:T(512)S(1)} %bitcast.93, f32[512,128]{1,0:T(8,128)S(1)} %copy.15), kind=kCustom, calls=%fused_computation.3.clone.1 | custom fusion | flops 65536 | bytes 788480 | tf_op jit(solution)/shard_map/while/body/eval_jaxpr/scatter-add | solution.py:55
  132.6 1.3 gather_fusion
  135.9 4.1 %scatter_fusion = f32[769,128]{1,0:T(8,128)S(1)} fusion(f32[769,128]{1,0:T(8,128)S(1)} %get-tuple-element.206, s32[512]{0:T(512)S(1)} %bitcast.93, f32[512,128]{1,0:T(8,128)S(1)} %copy.15), kind=kCustom, calls=%fused_computation.3.clone.1 | custom fusion | flops 65536 | bytes 788480 | tf_op jit(solution)/shard_map/while/body/eval_jaxpr/scatter-add | solution.py:55
  140.0 1.3 gather_fusion
  143.3 4.1 %scatter_fusion = f32[769,128]{1,0:T(8,128)S(1)} fusion(f32[769,128]{1,0:T(8,128)S(1)} %get-tuple-element.206, s32[512]{0:T(512)S(1)} %bitcast.93, f32[512,128]{1,0:T(8,128)S(1)} %copy.15), kind=kCustom, calls=%fused_computation.3.clone.1 | custom fusion | flops 65536 | bytes 788480 | tf_op jit(solution)/shard_map/while/body/eval_jaxpr/scatter-add | solution.py:55
  150.7 4.1 %scatter_fusion = f32[769,128]{1,0:T(8,128)S(1)} fusion(f32[769,128]{1,0:T(8,128)S(1)} %get-tuple-element.206, s32[512]{0:T(512)S(1)} %bitcast.93, f32[512,128]{1,0:T(8,128)S(1)} %copy.15), kind=kCustom, calls=%fused_computation.3.clone.1 | custom fusion | flops 65536 | bytes 788480 | tf_op jit(solution)/shard_map/while/body/eval_jaxpr/scatter-add | solution.py:55
  158.2 4.1 %scatter_fusion = f32[769,128]{1,0:T(8,128)S(1)} fusion(f32[769,128]{1,0:T(8,128)S(1)} %get-tuple-element.206, s32[512]{0:T(512)S(1)} %bitcast.93, f32[512,128]{1,0:T(8,128)S(1)} %copy.15), kind=kCustom, calls=%fused_computation.3.clone.1 | custom fusion | flops 65536 | bytes 788480 | tf_op jit(solution)/shard_map/while/body/eval_jaxpr/scatter-add | solution.py:55
  162.3 1.3 gather_fusion
  165.6 4.1 %scatter_fusion = f32[769,128]{1,0:T(8,128)S(1)} fusion(f32[769,128]{1,0:T(8,128)S(1)} %get-tuple-element.206, s32[512]{0:T(512)S(1)} %bitcast.93, f32[512,128]{1,0:T(8,128)S(1)} %copy.15), kind=kCustom, calls=%fused_computation.3.clone.1 | custom fusion | flops 65536 | bytes 788480 | tf_op jit(solution)/shard_map/while/body/eval_jaxpr/scatter-add | solution.py:55
  173.0 4.1 %scatter_fusion = f32[769,128]{1,0:T(8,128)S(1)} fusion(f32[769,128]{1,0:T(8,128)S(1)} %get-tuple-element.206, s32[512]{0:T(512)S(1)} %bitcast.93, f32[512,128]{1,0:T(8,128)S(1)} %copy.15), kind=kCustom, calls=%fused_computation.3.clone.1 | custom fusion | flops 65536 | bytes 788480 | tf_op jit(solution)/shard_map/while/body/eval_jaxpr/scatter-add | solution.py:55
  180.4 4.1 %scatter_fusion = f32[769,128]{1,0:T(8,128)S(1)} fusion(f32[769,128]{1,0:T(8,128)S(1)} %get-tuple-element.206, s32[512]{0:T(512)S(1)} %bitcast.93, f32[512,128]{1,0:T(8,128)S(1)} %copy.15), kind=kCustom, calls=%fused_computation.3.clone.1 | custom fusion | flops 65536 | bytes 788480 | tf_op jit(solution)/shard_map/while/body/eval_jaxpr/scatter-add | solution.py:55
  187.8 4.1 %scatter_fusion = f32[769,128]{1,0:T(8,128)S(1)} fusion(f32[769,128]{1,0:T(8,128)S(1)} %get-tuple-element.206, s32[512]{0:T(512)S(1)} %bitcast.93, f32[512,128]{1,0:T(8,128)S(1)} %copy.15), kind=kCustom, calls=%fused_computation.3.clone.1 | custom fusion | flops 65536 | bytes 788480 | tf_op jit(solution)/shard_map/while/body/eval_jaxpr/scatter-add | solution.py:55
  195.2 4.1 %scatter_fusion = f32[769,128]{1,0:T(8,128)S(1)} fusion(f32[769,128]{1,0:T(8,128)S(1)} %get-tuple-element.206, s32[512]{0:T(512)S(1)} %bitcast.93, f32[512,128]{1,0:T(8,128)S(1)} %copy.15), kind=kCustom, calls=%fused_computation.3.clone.1 | custom fusion | flops 65536 | bytes 788480 | tf_op jit(solution)/shard_map/while/body/eval_jaxpr/scatter-add | solution.py:55
  202.6 4.1 %scatter_fusion = f32[769,128]{1,0:T(8,128)S(1)} fusion(f32[769,128]{1,0:T(8,128)S(1)} %get-tuple-element.206, s32[512]{0:T(512)S(1)} %bitcast.93, f32[512,128]{1,0:T(8,128)S(1)} %copy.15), kind=kCustom, calls=%fused_computation.3.clone.1 | custom fusion | flops 65536 | bytes 788480 | tf_op jit(solution)/shard_map/while/body/eval_jaxpr/scatter-add | solution.py:55
  206.8 1.3 gather_fusion
  210.1 4.1 %scatter_fusion = f32[769,128]{1,0:T(8,128)S(1)} fusion(f32[769,128]{1,0:T(8,128)S(1)} %get-tuple-element.206, s32[512]{0:T(512)S(1)} %bitcast.93, f32[512,128]{1,0:T(8,128)S(1)} %copy.15), kind=kCustom, calls=%fused_computation.3.clone.1 | custom fusion | flops 65536 | bytes 788480 | tf_op jit(solution)/shard_map/while/body/eval_jaxpr/scatter-add | solution.py:55
  217.5 4.1 %scatter_fusion = f32[769,128]{1,0:T(8,128)S(1)} fusion(f32[769,128]{1,0:T(8,128)S(1)} %get-tuple-element.206, s32[512]{0:T(512)S(1)} %bitcast.93, f32[512,128]{1,0:T(8,128)S(1)} %copy.15), kind=kCustom, calls=%fused_computation.3.clone.1 | custom fusion | flops 65536 | bytes 788480 | tf_op jit(solution)/shard_map/while/body/eval_jaxpr/scatter-add | solution.py:55
  222.9 4.5 %collective-permute-start.3 = (f32[1,128,128]{2,1,0:T(8,128)S(1)}, f32[1,128,128]{2,1,0:T(8,128)S(1)}, u32[]{:S(2)}, u32[]{:S(2)}) collective-permute-start(f32[1,128,128]{2,1,0:T(8,128)S(1)} %get-tuple-element.113), channel_id=1, source_target_pairs={{0,2},{2,4},{4,6},{6,8},{8,10},{10,12},{12,14},{14,16},{16,18},{18... | collective-permute-start | bytes 196616 | tf_op jit(solution)/shard_map/ppermute | solution.py:14
  227.5 64.0 %while.24 = (s32[]{:T(128)}, f32[512,128]{1,0:T(8,128)S(1)}, s32[27,512]{1,0:T(8,128)S(1)}, bf16[769,128]{1,0:T(8,128)(2,1)S(1)}, bf16[27,128,128]{2,1,0:T(8,128)(2,1)}, /*index=5*/s32[]{:T(128)}, s32[]{:T(128)}) while((s32[]{:T(128)}, f32[512,128]{1,0:T(8,128)S(1)}, s32[27,512]{1,0:T(8,128)S(1)}, bf16[769,128]{1,0:T(8,128)(2,1)S(1)}, ...), condition=%wide.region_1.2_spmd.clone, body=%wide.region_0.1_spmd.clone.sunk | while | flops 16910852 | bytes 963163 | solution.py:42
  241.7 1.3 gather_fusion.1
  246.5 1.3 gather_fusion.1
  248.8 1.3 gather_fusion.1
  253.6 1.3 gather_fusion.1
  263.1 1.3 gather_fusion.1
  267.8 1.3 gather_fusion.1
  270.2 1.3 gather_fusion.1
  277.3 1.3 gather_fusion.1
  282.1 1.3 gather_fusion.1
  284.4 1.3 gather_fusion.1
  289.2 1.3 gather_fusion.1
  295.2 67.4 %all-reduce.3.cloned.1.call-done = f32[3456,128]{1,0:T(8,128)} async-done(((f32[3456,128]{1,0:T(8,128)}), f32[3456,128]{1,0:T(8,128)}) %all-reduce.3.cloned.1.call-update) | async-done | bytes 1769488 | tf_op jit(solution)/shard_map/psum | solution.py:75
  362.5 2.8 broadcast_multiply_fusion
  (268 shorter events, 121.9 us)
Async XLA Ops:
  7.2 355.4 %all-reduce.3.cloned.1.call-start = ((), (), s32[]{:S(2)}) async-start(), calls=%async_computation | async-start | bytes 3538944 | tf_op jit(solution)/shard_map/psum | solution.py:75
  10.5 7.7 %collective-permute-start = (bf16[1,128,128]{2,1,0:T(8,128)(2,1)S(1)}, bf16[1,128,128]{2,1,0:T(8,128)(2,1)S(1)}, u32[]{:S(2)}, u32[]{:S(2)}) collective-permute-start(bf16[1,128,128]{2,1,0:T(8,128)(2,1)S(1)} %get-tuple-element.115), channel_id=1, source_target_pairs={{0,2},{2,4},{4,6},{6,8},{8,10},{10,12},{12,14},{14,16},{16,18},{18... | collective-permute-start | bytes 98312 | tf_op jit(solution)/shard_map/ppermute | solution.py:14
  15.4 5.8 %collective-permute-start.1 = (bf16[1,128,128]{2,1,0:T(8,128)(2,1)S(1)}, bf16[1,128,128]{2,1,0:T(8,128)(2,1)S(1)}, u32[]{:S(2)}, u32[]{:S(2)}) collective-permute-start(bf16[1,128,128]{2,1,0:T(8,128)(2,1)S(1)} %get-tuple-element.116), channel_id=1, source_target_pairs={{2,0},{4,2},{6,4},{8,6},{10,8},{12,10},{14,12},{16,14},{18,16},{20... | collective-permute-start | bytes 98312 | tf_op jit(solution)/shard_map/ppermute | solution.py:15
  221.6 70.1 %collective-permute-start.2 = (f32[1,128,128]{2,1,0:T(8,128)S(1)}, f32[1,128,128]{2,1,0:T(8,128)S(1)}, u32[]{:S(2)}, u32[]{:S(2)}) collective-permute-start(f32[1,128,128]{2,1,0:T(8,128)S(1)} %get-tuple-element.114), channel_id=1, source_target_pairs={{2,0},{4,2},{6,4},{8,6},{10,8},{12,10},{14,12},{16,14},{18,16},{20... | collective-permute-start | bytes 196616 | tf_op jit(solution)/shard_map/ppermute | solution.py:15
  222.9 70.1 %collective-permute-start.3 = (f32[1,128,128]{2,1,0:T(8,128)S(1)}, f32[1,128,128]{2,1,0:T(8,128)S(1)}, u32[]{:S(2)}, u32[]{:S(2)}) collective-permute-start(f32[1,128,128]{2,1,0:T(8,128)S(1)} %get-tuple-element.113), channel_id=1, source_target_pairs={{0,2},{2,4},{4,6},{6,8},{8,10},{10,12},{12,14},{14,16},{16,18},{18... | collective-permute-start | bytes 196616 | tf_op jit(solution)/shard_map/ppermute | solution.py:14
  227.4 64.1 %copy-start = (pred[513]{0:T(1024)(128)(4,1)S(1)}, pred[513]{0:T(1024)(128)(4,1)}, u32[]{:S(2)}) copy-start(pred[513]{0:T(1024)(128)(4,1)} %constant.26.clone.1) | copy-start | bytes 1543
Sparse Core Ops, SparseCore 0:
  227.6 134.9 all-reduce.2
where the time goes:
time: 377 us; the launch traced here: 372 us
  other arithmetic  120 us (32%)
  local copies, waits for them, and re-layouts  77.3 us (21%)
  matrix products  74.8 us (20%)
  waiting for transfers between devices  70.3 us (19%)
  between operations  14.8 us (4%)
  starting transfers between devices  12 us (3%)
    scatter-add x27, other arithmetic, backward_step(): return (accum_grad.at[source].add(contrib), weight_part)  110 us
    psum x1, waiting for transfers between devices, per_device(): summed = lax.psum(flat_parts, ('space', 'batch'))  67.4 us
    gather x27, local copies, waits for them, and re-layouts, forward_step(): extended[source]  36.2 us
    gather x27, local copies, waits for them, and re-layouts, backward_step(): gathered = extended[source]  36.2 us
    dot_general x27, matrix products, forward_step(): jnp.dot(extended[source], weight, preferred_element_type=jnp.float32)  26 us
    dot_general x27, matrix products, backward_step(): contrib = jnp.dot(grad_rows, weight.T, preferred_element_type=jnp.float32)  25.4 us
    dot_general x27, matrix products, backward_step(): lax.dot_general(gathered, grad_rows, (((0,), (0,)), ((), ())), preferred_...  23.3 us
    ppermute x2, starting transfers between devices, with_halo(): before = lax.ppermute(last, axis, up)  9.39 us
  transfers between devices with their start and end apart: 5, of which 2 were waited for; matrix products, arithmetic and copies ran while one was open for 18% of the time, Pallas kernels for 0%

commit v1 on v0

v1 whole, which is shorter than its diff:
```python
import functools

import jax
import jax.numpy as jnp
from jax import lax
from jax.experimental import pallas as pl
from jax.experimental.pallas import tpu as pltpu
from jax.sharding import PartitionSpec as P

F32 = jnp.float32
BF16 = jnp.bfloat16
MESH = pl.DeviceIdType.MESH
GROUPS = 3
BATCH = 3
TILES = 16
ROW = 8


def dot(a, b, contract=((1,), (0,))):
    return lax.dot_general(a, b, (contract, ((), ())), preferred_element_type=F32)


def onehot_columns(row, height):
    line = lax.broadcasted_iota(jnp.int32, (height, row.shape[1]), 0)
    return jnp.where(line == row, jnp.ones((), F32), jnp.zeros((), F32)).astype(BF16)


def split_pair(x):
    high = x.astype(BF16)
    low = (x - high.astype(F32)).astype(BF16)
    return jnp.concatenate([high, low], 1)


def mesh_bits(n_space, n_batch):
    bits = [("batch", 1)] if n_batch > 1 else []
    weight = 1
    while weight < n_space:
        bits.append(("space", weight))
        weight *= 2
    weight = 2
    while weight < n_batch:
        bits.append(("batch", weight))
        weight *= 2
    return bits


def plan(n_space, n_batch):
    bits = mesh_bits(n_space, n_batch)
    halvings = min(4, len(bits))
    orders = []
    for q in range(GROUPS):
        rest = bits[1:halvings]
        turn = q % max(len(rest), 1)
        orders.append(bits[:1] + rest[turn:] + rest[:turn])
    return orders, bits[halvings:]


def kernel(
    n_space, n_batch, scale,
    feat, w, kmap, send, count, cot,
    out, gfeat, gw,
    ext, outgoing, extt, grad, gt, dw, inbox, acc, gext, back, outt,
    halo_send, halo_recv, back_send, back_recv, sum_send, sum_recv,
):
    offsets, channels = w.shape[0], w.shape[1]
    slots = feat.shape[0]
    halo = send.shape[1]
    table = slots + 2 * halo
    per_group = offsets // GROUPS
    here = {"space": lax.axis_index("space"), "batch": lax.axis_index("batch")}
    s = here["space"]
    orders, full = plan(n_space, n_batch)
    halvings = len(orders[0])

    def bit_of(bit):
        return (here[bit[0]] // bit[1]) % 2

    def partner(bit):
        return {**here, bit[0]: here[bit[0]] + bit[1] * (1 - 2 * bit_of(bit))}

    lower = {**here, "space": s - 1}
    upper = {**here, "space": s + 1}
    has_lower = s > 0
    has_upper = s < n_space - 1

    barrier = pltpu.get_barrier_semaphore()
    for bit in orders[0] + full:
        pl.semaphore_signal(barrier, inc=1, device_id=partner(bit), device_id_type=MESH)

    @pl.when(has_lower)
    def _():
        pl.semaphore_signal(barrier, inc=1, device_id=lower, device_id_type=MESH)

    @pl.when(has_upper)
    def _():
        pl.semaphore_signal(barrier, inc=1, device_id=upper, device_id_type=MESH)

    alive = lax.broadcasted_iota(jnp.int32, (slots, channels), 0) < count[0, 0]
    live = jnp.where(alive, feat[...].astype(F32), jnp.zeros((), F32)).astype(BF16)
    ext[:slots] = live
    grad[...] = jnp.where(alive, cot[...].astype(F32), jnp.zeros((), F32)).astype(BF16)
    lists = jnp.concatenate([send[0:1, :], send[1:2, :]], 1)
    outgoing[...] = dot(onehot_columns(lists, slots), live, ((0,), (0,))).astype(BF16)

    @pl.when(s == 0)
    def _():
        ext[slots : slots + halo] = jnp.zeros((halo, channels), BF16)
        back[halo:] = jnp.zeros((halo, channels), F32)

    @pl.when(s == n_space - 1)
    def _():
        ext[slots + halo :] = jnp.zeros((halo, channels), BF16)
        back[:halo] = jnp.zeros((halo, channels), F32)

    neighbours = 1 * (jnp.minimum(s, 1) + jnp.minimum(n_space - 1 - s, 1))
    pl.semaphore_wait(barrier, len(orders[0] + full) + neighbours)

    to_lower = pltpu.make_async_remote_copy(
        src_ref=outgoing.at[:halo], dst_ref=ext.at[pl.ds(slots + halo, halo)],
        send_sem=halo_send.at[0], recv_sem=halo_recv.at[0], device_id=lower, device_id_type=MESH)
    to_upper = pltpu.make_async_remote_copy(
        src_ref=outgoing.at[pl.ds(halo, halo)], dst_ref=ext.at[pl.ds(slots, halo)],
        send_sem=halo_send.at[1], recv_sem=halo_recv.at[1], device_id=upper, device_id_type=MESH)

    def start_both(down, up):
        @pl.when(has_lower)
        def _():
            down.start()

        @pl.when(has_upper)
        def _():
            up.start()

    def wait_both(down, up):
        @pl.when(has_lower)
        def _():
            down.wait_send()
            up.wait_recv()

        @pl.when(has_upper)
        def _():
            up.wait_send()
            down.wait_recv()

    start_both(to_lower, to_upper)

    steps = halvings + len(full) + halvings
    place = [0] * GROUPS
    begin = [[0] for _ in range(GROUPS)]
    flying = [None] * GROUPS

    def launch(q):
        step = place[q]
        ks = pl.ds(q * per_group, per_group)
        sem = q * steps + step
        if step < halvings:
            bit = orders[q][step]
            size = TILES >> (step + 1)
            src = dw.at[ks, pl.ds(begin[q][-1] + (1 - bit_of(bit)) * size, size)]
            dst = inbox.at[ks, pl.ds(TILES - 2 * size, size)]
        elif step < halvings + len(full):
            bit = full[step - halvings]
            size = TILES >> halvings
            src = dw.at[ks, pl.ds(begin[q][-1], size)]
            dst = inbox.at[ks, pl.ds(TILES - size + (step - halvings) * size, size)]
        else:
            level = steps - 1 - step
            bit = orders[q][level]
            size = TILES >> (level + 1)
            src = gw.at[ks, pl.ds(begin[q][level + 1], size)]
            dst = gw.at[ks, pl.ds(begin[q][level + 1], size)]
        flying[q] = pltpu.make_async_remote_copy(
            src_ref=src, dst_ref=dst, send_sem=sum_send.at[sem], recv_sem=sum_recv.at[sem],
            device_id=partner(bit), device_id_type=MESH)
        flying[q].start()

    def advance(q):
        step = place[q]
        if step >= steps:
            return
        flying[q].wait()
        ks = pl.ds(q * per_group, per_group)
        if step < halvings + len(full):
            if step < halvings:
                size = TILES >> (step + 1)
                at = begin[q][-1] + bit_of(orders[q][step]) * size
                begin[q].append(at)
                got = pl.ds(TILES - 2 * size, size)
            else:
                size = TILES >> halvings
                at = begin[q][-1]
                got = pl.ds(TILES - size + (step - halvings) * size, size)
            mine = pl.ds(at, size)
            total = dw[ks, mine] + inbox[ks, got]
            if step == halvings + len(full) - 1:
                gw[ks, mine] = total * scale
            else:
                dw[ks, mine] = total
        place[q] = step + 1
        if place[q] < steps:
            launch(q)

    def advance_all():
        for q in range(GROUPS):
            advance(q)

    acc[...] = jnp.zeros_like(acc)
    outt[...] = jnp.zeros_like(outt)
    wait_both(to_lower, to_upper)
    extt[...] = ext[...].astype(F32).T.astype(BF16)

    def weight_step(j, carry):
        for t in range(BATCH):
            k = j * BATCH + t
            picked = onehot_columns(kmap[pl.ds(k, 1), :], table)
            gathered = dot(extt[...], picked).astype(BF16)
            gt[pl.ds(pl.multiple_of(k * channels, channels), channels)] = gathered
            dw[k] = dot(gathered, grad[...]).reshape(TILES, ROW, channels)
        return carry

    def scatter_step(j, carry):
        weights = w[pl.ds(j * BATCH, BATCH)].reshape(BATCH * channels, channels)
        contrib = dot(grad[...], weights, ((1,), (1,)))
        picks, parts = [], []
        for t in range(BATCH):
            picks.append(onehot_columns(kmap[pl.ds(j * BATCH + t, 1), :], table))
            parts.append(split_pair(contrib[:, t * channels : (t + 1) * channels]))
        acc[...] += dot(jnp.concatenate(picks, 1), jnp.concatenate(parts, 0))
        return carry

    def forward_step(j, carry):
        weights = w[pl.ds(j * BATCH, BATCH)].reshape(BATCH * channels, channels)
        size = BATCH * channels
        rows = gt[pl.ds(pl.multiple_of(j * size, size), size)]
        outt[...] += dot(weights, rows, ((0,), (0,)))
        return carry

    loops = per_group // BATCH
    for q in range(GROUPS):
        lax.fori_loop(q * loops, (q + 1) * loops, weight_step, 0)
        for earlier in range(q):
            advance(earlier)
        launch(q)

    total_loops = offsets // BATCH
    for j in range(0, total_loops, 2):
        lax.fori_loop(j, min(j + 2, total_loops), scatter_step, 0)
        advance_all()

    both = acc[...]
    gext[...] = both[:, :channels] + both[:, channels:]
    back_lower = pltpu.make_async_remote_copy(
        src_ref=gext.at[pl.ds(slots, halo)], dst_ref=back.at[:halo],
        send_sem=back_send.at[0], recv_sem=back_recv.at[0], device_id=lower, device_id_type=MESH)
    back_upper = pltpu.make_async_remote_copy(
        src_ref=gext.at[pl.ds(slots + halo, halo)], dst_ref=back.at[pl.ds(halo, halo)],
        send_sem=back_send.at[1], recv_sem=back_recv.at[1], device_id=upper, device_id_type=MESH)
    start_both(back_lower, back_upper)

    lax.fori_loop(0, total_loops, forward_step, 0)
    out[...] = jnp.where(alive, outt[...].T, jnp.zeros((), F32)).astype(BF16)
    advance_all()

    wait_both(back_lower, back_upper)
    lists = jnp.concatenate([send[1:2, :], send[0:1, :]], 1)
    extra = dot(onehot_columns(lists, slots), split_pair(back[...]))
    local = gext[:slots] + extra[:, :channels] + extra[:, channels:]
    gfeat[...] = jnp.where(alive, local, jnp.zeros((), F32)).astype(BF16)

    while min(place) < steps:
        advance_all()


def per_device(n_space, n_batch, features, weights, kernel_map, send_rows, counts, cotangent):
    slots, channels = features.shape[1], features.shape[2]
    offsets = weights.shape[0]
    halo = send_rows.shape[2]
    table = slots + 2 * halo
    orders, full = plan(n_space, n_batch)
    steps = 2 * len(orders[0]) + len(full)
    vmem = pl.BlockSpec(memory_space=pltpu.VMEM)
    smem = pl.BlockSpec(memory_space=pltpu.SMEM)
    scale = float((slots * n_space * n_batch) ** -0.5)
    result, grad_features, grad_weights = pl.pallas_call(
        functools.partial(kernel, n_space, n_batch, scale),
        out_shape=(
            jax.ShapeDtypeStruct((slots, channels), BF16),
            jax.ShapeDtypeStruct((slots, channels), BF16),
            jax.ShapeDtypeStruct((offsets, TILES, ROW, channels), F32),
        ),
        in_specs=[vmem, vmem, vmem, vmem, smem, vmem],
        out_specs=(vmem, vmem, vmem),
        scratch_shapes=[
            pltpu.VMEM((table, channels), BF16),
            pltpu.VMEM((2 * halo, channels), BF16),
            pltpu.VMEM((channels, table), BF16),
            pltpu.VMEM((slots, channels), BF16),
            pltpu.VMEM((offsets * channels, slots), BF16),
            pltpu.VMEM((offsets, TILES, ROW, channels), F32),
            pltpu.VMEM((offsets, TILES + len(full), ROW, channels), F32),
            pltpu.VMEM((table, 2 * channels), F32),
            pltpu.VMEM((table, channels), F32),
            pltpu.VMEM((2 * halo, channels), F32),
            pltpu.VMEM((channels, slots), F32),
            pltpu.SemaphoreType.DMA((2,)),
            pltpu.SemaphoreType.DMA((2,)),
            pltpu.SemaphoreType.DMA((2,)),
            pltpu.SemaphoreType.DMA((2,)),
            pltpu.SemaphoreType.DMA((GROUPS * steps,)),
            pltpu.SemaphoreType.DMA((GROUPS * steps,)),
        ],
        compiler_params=pltpu.CompilerParams(
            collective_id=0, has_side_effects=True, vmem_limit_bytes=48 * 1024 * 1024
        ),
        name="sparse_conv",
    )(features[0], weights, kernel_map[0], send_rows[0], counts, cotangent[0])
    return (
        result[None],
        grad_features[None],
        grad_weights.reshape(offsets, channels, channels),
    )


def solution(mesh):
    in_specs = (
        P("batch", "space", None),
        P(),
        P("batch", None, "space"),
        P("batch", None, "space"),
        P("batch", "space"),
        P("batch", "space", None),
    )
    out_specs = (P("batch", "space", None), P("batch", "space", None), P())
    body = functools.partial(per_device, mesh.shape["space"], mesh.shape["batch"])
    return jax.shard_map(body, mesh=mesh, in_specs=in_specs, out_specs=out_specs, check_vma=False)
```

time: 377 us -> 61.5 us (0.16); the launches traced: 372 us -> 61.2 us
  other arithmetic: 120 us -> 0 us
  matrix products: 74.8 us -> 0 us
  local copies, waits for them, and re-layouts: 77.3 us -> 6.99 us
  waiting for transfers between devices: 70.3 us -> 0 us
  Pallas kernels: 0 us -> 52.9 us
  between operations: 14.8 us -> 1.29 us
  starting transfers between devices: 12 us -> 0 us
    scatter-add x29 -> x0, other arithmetic: 112 us -> none  [the longest x27 110 us: backward_step(): return (accum_grad.at[source].add(contrib), weight_part)]
    dot_general x81 -> x0, matrix products: 74.8 us -> none  [the longest x27 26 us: forward_step(): jnp.dot(extended[source], weight, preferred_element_type=jnp.float32)]
    gather x55 -> x0, local copies, waits for them, and re-layouts: 73.2 us -> none  [the longest x27 36.2 us: forward_step(): extended[source]]
    psum x1 -> x0, waiting for transfers between devices: 67.4 us -> none  [per_device(): summed = lax.psum(flat_parts, ('space', 'batch'))]
    pallas_call x0 -> x1, Pallas kernels: none -> 52.9 us  [per_device(): pl.pallas_call(functools.partial(kernel, n_space, n_batch, scale), out_sh...]
    ppermute x4 -> x0, starting transfers between devices: 12 us -> none  [the longest x2 9.39 us: with_halo(): before = lax.ppermute(last, axis, up)]
    unnamed x3 -> x12, local copies, waits for them, and re-layouts: 0.83 us -> 6.99 us
  transfers between devices with their start and end apart: 5 -> 0, of which waited for: 2 -> 0; matrix products, arithmetic and copies ran while one was open for 18% -> 0% of each run, Pallas kernels for 0% -> 0%
where the time goes in v1:
time: 61.5 us; the launch traced here: 61.2 us
  Pallas kernels  52.9 us (86%)
  local copies, waits for them, and re-layouts  6.99 us (11%)
  between operations  1.29 us (2%)
    pallas_call x1, Pallas kernels, per_device(): pl.pallas_call(functools.partial(kernel, n_space, n_batch, scale), out_sh...  52.9 us
    unnamed x12, local copies, waits for them, and re-layouts  6.99 us

profile of v1, /device:TPU:0, one launch (start us, length us, event | category | flops | bytes accessed | tf_op | source)
XLA Modules:
  0.0 61.2 jit_solution(11257992621085409512)
XLA Ops:
  1.3 0.8 %copy.11 = s32[1,27,512]{2,1,0:T(8,128)S(1)} copy(s32[1,27,512]{2,0,1:T(1,128)} %param.8) | data formatting | bytes 110592
  2.1 0.0 copy-start
  2.1 1.2 %copy-done = bf16[27,128,128]{2,1,0:T(8,128)(2,1)S(1)} copy-done((bf16[27,128,128]{2,1,0:T(8,128)(2,1)S(1)}, bf16[27,128,128]{2,1,0:T(8,128)(2,1)}, u32[]{:S(2)}) %copy-start) | copy-done | bytes 884760
  3.3 0.0 copy-start.1
  3.3 0.9 %copy-done.1 = bf16[1,512,128]{2,1,0:T(8,128)(2,1)S(1)} copy-done((bf16[1,512,128]{2,1,0:T(8,128)(2,1)S(1)}, bf16[1,512,128]{2,1,0:T(8,128)(2,1)}, u32[]{:S(2)}) %copy-start.1) | copy-done | bytes 131096
  4.2 0.0 copy-start.2
  4.2 0.9 %copy-done.2 = bf16[1,512,128]{2,1,0:T(8,128)(2,1)S(1)} copy-done((bf16[1,512,128]{2,1,0:T(8,128)(2,1)S(1)}, bf16[1,512,128]{2,1,0:T(8,128)(2,1)}, u32[]{:S(2)}) %copy-start.2) | copy-done | bytes 131096
  5.1 0.0 copy-start.3
  5.1 0.7 %copy-done.3 = s32[1,2,128]{2,1,0:T(2,128)S(1)} copy-done((s32[1,2,128]{2,1,0:T(2,128)S(1)}, s32[1,2,128]{2,1,0:T(2,128)}, u32[]{:S(2)}) %copy-start.3) | copy-done | bytes 1048
  5.8 52.9 %sparse_conv.1 = (bf16[512,128]{1,0:T(8,128)(2,1)S(1)}, bf16[512,128]{1,0:T(8,128)(2,1)S(1)}, f32[27,16,8,128]{3,2,1,0:T(8,128)S(1)}) custom-call(bf16[512,128]{1,0:T(8,128)(2,1)S(1)} %bitcast.11, bf16[27,128,128]{2,1,0:T(8,128)(2,1)S(1)} %copy-done, s32[27,512]{1,0:T(8,128)S(1)} %bitcast.10, s32[2,128]{1,0:T(2,128)S(1)} %bitcast.15, ...), custom_call_target="tpu_custom_call" | custom-call | tf_op jit(solution)/shard_map/sparse_conv/pallas_call | solution.py:284
  58.7 0.7 %copy.16 = bf16[1,512,128]{2,1,0:T(8,128)(2,1)} copy(bf16[1,512,128]{2,1,0:T(8,128)(2,1)S(1)} %bitcast.14) | data formatting | bytes 262144
  59.3 0.7 %copy.17 = bf16[1,512,128]{2,1,0:T(8,128)(2,1)} copy(bf16[1,512,128]{2,1,0:T(8,128)(2,1)S(1)} %bitcast.13) | data formatting | bytes 262144
  60.0 1.2 %copy.18 = f32[27,128,128]{2,1,0:T(8,128)} copy(f32[27,128,128]{2,1,0:T(8,128)S(1)} %bitcast.9) | data formatting | bytes 3538944
Async XLA Ops:
  2.1 1.2 %copy-start = (bf16[27,128,128]{2,1,0:T(8,128)(2,1)S(1)}, bf16[27,128,128]{2,1,0:T(8,128)(2,1)}, u32[]{:S(2)}) copy-start(bf16[27,128,128]{2,1,0:T(8,128)(2,1)} %w.1) | copy-start | bytes 2654212
  3.3 0.9 %copy-start.1 = (bf16[1,512,128]{2,1,0:T(8,128)(2,1)S(1)}, bf16[1,512,128]{2,1,0:T(8,128)(2,1)}, u32[]{:S(2)}) copy-start(bf16[1,512,128]{2,1,0:T(8,128)(2,1)} %param.6) | copy-start | bytes 393220
  4.2 0.9 %copy-start.2 = (bf16[1,512,128]{2,1,0:T(8,128)(2,1)S(1)}, bf16[1,512,128]{2,1,0:T(8,128)(2,1)}, u32[]{:S(2)}) copy-start(bf16[1,512,128]{2,1,0:T(8,128)(2,1)} %param.11) | copy-start | bytes 393220
  5.1 0.7 %copy-start.3 = (s32[1,2,128]{2,1,0:T(2,128)S(1)}, s32[1,2,128]{2,1,0:T(2,128)}, u32[]{:S(2)}) copy-start(s32[1,2,128]{2,1,0:T(2,128)} %param.9) | copy-start | bytes 3076

commit v2 on v1

--- a/solution.py
+++ b/solution.py
@@ -10,8 +10,10 @@
 F32 = jnp.float32
 BF16 = jnp.bfloat16
 MESH = pl.DeviceIdType.MESH
-GROUPS = 3
 BATCH = 3
+SIZES = (4, 3, 2)
+GROUPS = len(SIZES)
+EARLY = 2
 TILES = 16
 ROW = 8
 
@@ -21,8 +23,9 @@
 
 
 def onehot_columns(row, height):
-    line = lax.broadcasted_iota(jnp.int32, (height, row.shape[1]), 0)
-    return jnp.where(line == row, jnp.ones((), F32), jnp.zeros((), F32)).astype(BF16)
+    line = lax.broadcasted_iota(jnp.int16, (height, row.shape[1]), 0)
+    hit = line == jnp.broadcast_to(row.astype(jnp.int16), line.shape)
+    return jnp.where(hit, jnp.ones((), BF16), jnp.zeros((), BF16))
 
 
 def split_pair(x):
@@ -57,8 +60,9 @@
 
 def kernel(
     n_space, n_batch, scale,
-    feat, w, kmap, send, count, cot,
+    feat_hbm, w_hbm, kmap_hbm, send_hbm, count, cot_hbm,
     out, gfeat, gw,
+    feat, w, kmap, send, cot, load_sem,
     ext, outgoing, extt, grad, gt, dw, inbox, acc, gext, back, outt,
     halo_send, halo_recv, back_send, back_recv, sum_send, sum_recv,
 ):
@@ -66,7 +70,7 @@
     slots = feat.shape[0]
     halo = send.shape[1]
     table = slots + 2 * halo
-    per_group = offsets // GROUPS
+    firsts = [BATCH * sum(SIZES[:q]) for q in range(GROUPS)]
     here = {"space": lax.axis_index("space"), "batch": lax.axis_index("batch")}
     s = here["space"]
     orders, full = plan(n_space, n_batch)
@@ -83,6 +87,12 @@
     has_lower = s > 0
     has_upper = s < n_space - 1
 
+    loads = {}
+    pairs = dict(feat=(feat_hbm, feat), send=(send_hbm, send), cot=(cot_hbm, cot), kmap=(kmap_hbm, kmap), w=(w_hbm, w))
+    for n, (name, (src, dst)) in enumerate(pairs.items()):
+        loads[name] = pltpu.make_async_copy(src, dst, load_sem.at[n])
+        loads[name].start()
+
     barrier = pltpu.get_barrier_semaphore()
     for bit in orders[0] + full:
         pl.semaphore_signal(barrier, inc=1, device_id=partner(bit), device_id_type=MESH)
@@ -96,9 +106,10 @@
         pl.semaphore_signal(barrier, inc=1, device_id=upper, device_id_type=MESH)
 
     alive = lax.broadcasted_iota(jnp.int32, (slots, channels), 0) < count[0, 0]
+    loads["feat"].wait()
     live = jnp.where(alive, feat[...].astype(F32), jnp.zeros((), F32)).astype(BF16)
     ext[:slots] = live
-    grad[...] = jnp.where(alive, cot[...].astype(F32), jnp.zeros((), F32)).astype(BF16)
+    loads["send"].wait()
     lists = jnp.concatenate([send[0:1, :], send[1:2, :]], 1)
     outgoing[...] = dot(onehot_columns(lists, slots), live, ((0,), (0,))).astype(BF16)
 
@@ -151,7 +162,7 @@
 
     def launch(q):
         step = place[q]
-        ks = pl.ds(q * per_group, per_group)
+        ks = pl.ds(firsts[q], BATCH * SIZES[q])
         sem = q * steps + step
         if step < halvings:
             bit = orders[q][step]
@@ -179,7 +190,7 @@
         if step >= steps:
             return
         flying[q].wait()
-        ks = pl.ds(q * per_group, per_group)
+        ks = pl.ds(firsts[q], BATCH * SIZES[q])
         if step < halvings + len(full):
             if step < halvings:
                 size = TILES >> (step + 1)
@@ -206,26 +217,31 @@
 
     acc[...] = jnp.zeros_like(acc)
     outt[...] = jnp.zeros_like(outt)
-    wait_both(to_lower, to_upper)
-    extt[...] = ext[...].astype(F32).T.astype(BF16)
-
-    def weight_step(j, carry):
-        for t in range(BATCH):
-            k = j * BATCH + t
-            picked = onehot_columns(kmap[pl.ds(k, 1), :], table)
-            gathered = dot(extt[...], picked).astype(BF16)
-            gt[pl.ds(pl.multiple_of(k * channels, channels), channels)] = gathered
-            dw[k] = dot(gathered, grad[...]).reshape(TILES, ROW, channels)
-        return carry
-
+    loads["cot"].wait()
+    grad[...] = jnp.where(alive, cot[...].astype(F32), jnp.zeros((), F32)).astype(BF16)
+    loads["kmap"].wait()
+    loads["w"].wait()
     def scatter_step(j, carry):
         weights = w[pl.ds(j * BATCH, BATCH)].reshape(BATCH * channels, channels)
         contrib = dot(grad[...], weights, ((1,), (1,)))
         picks, parts = [], []
         for t in range(BATCH):
-            picks.append(onehot_columns(kmap[pl.ds(j * BATCH + t, 1), :], table))
+            picks.append(onehot_columns(kmap[j * BATCH + t], table))
             parts.append(split_pair(contrib[:, t * channels : (t + 1) * channels]))
         acc[...] += dot(jnp.concatenate(picks, 1), jnp.concatenate(parts, 0))
+        return carry
+
+    lax.fori_loop(0, EARLY, scatter_step, 0)
+    wait_both(to_lower, to_upper)
+    extt[...] = ext[...].astype(F32).T.astype(BF16)
+
+    def weight_step(j, carry):
+        for t in range(BATCH):
+            k = j * BATCH + t
+            picked = onehot_columns(kmap[k], table)
+            gathered = dot(extt[...], picked).astype(BF16)
+            gt[pl.ds(pl.multiple_of(k * channels, channels), channels)] = gathered
+            dw[k] = dot(gathered, grad[...]).reshape(TILES, ROW, channels)
         return carry
 
     def forward_step(j, carry):
@@ -235,16 +251,20 @@
         outt[...] += dot(weights, rows, ((0,), (0,)))
         return carry
 
-    loops = per_group // BATCH
-    for q in range(GROUPS):
-        lax.fori_loop(q * loops, (q + 1) * loops, weight_step, 0)
-        for earlier in range(q):
-            advance(earlier)
-        launch(q)
-
     total_loops = offsets // BATCH
-    for j in range(0, total_loops, 2):
-        lax.fori_loop(j, min(j + 2, total_loops), scatter_step, 0)
+    lax.fori_loop(0, 4, weight_step, 0)
+    launch(0)
+    lax.fori_loop(4, 5, weight_step, 0)
+    advance(0)
+    lax.fori_loop(5, 7, weight_step, 0)
+    launch(1)
+    lax.fori_loop(7, 8, weight_step, 0)
+    advance(0)
+    advance(1)
+    lax.fori_loop(8, total_loops, weight_step, 0)
+    launch(2)
+    for j in range(EARLY, total_loops):
+        lax.fori_loop(j, j + 1, scatter_step, 0)
         advance_all()
 
     both = acc[...]
@@ -257,7 +277,9 @@
         send_sem=back_send.at[1], recv_sem=back_recv.at[1], device_id=upper, device_id_type=MESH)
     start_both(back_lower, back_upper)
 
-    lax.fori_loop(0, total_loops, forward_step, 0)
+    lax.fori_loop(0, 5, forward_step, 0)
+    advance_all()
+    lax.fori_loop(5, total_loops, forward_step, 0)
     out[...] = jnp.where(alive, outt[...].T, jnp.zeros((), F32)).astype(BF16)
     advance_all()
 
@@ -278,6 +300,7 @@
     table = slots + 2 * halo
     orders, full = plan(n_space, n_batch)
     steps = 2 * len(orders[0]) + len(full)
+    hbm = pl.BlockSpec(memory_space=pltpu.HBM)
     vmem = pl.BlockSpec(memory_space=pltpu.VMEM)
     smem = pl.BlockSpec(memory_space=pltpu.SMEM)
     scale = float((slots * n_space * n_batch) ** -0.5)
@@ -288,9 +311,15 @@
             jax.ShapeDtypeStruct((slots, channels), BF16),
             jax.ShapeDtypeStruct((offsets, TILES, ROW, channels), F32),
         ),
-        in_specs=[vmem, vmem, vmem, vmem, smem, vmem],
+        in_specs=[hbm, hbm, hbm, hbm, smem, hbm],
         out_specs=(vmem, vmem, vmem),
         scratch_shapes=[
+            pltpu.VMEM((slots, channels), BF16),
+            pltpu.VMEM((offsets, channels, channels), BF16),
+            pltpu.VMEM((offsets, 1, slots), jnp.int32),
+            pltpu.VMEM((2, halo), jnp.int32),
+            pltpu.VMEM((slots, channels), BF16),
+            pltpu.SemaphoreType.DMA((5,)),
             pltpu.VMEM((table, channels), BF16),
             pltpu.VMEM((2 * halo, channels), BF16),
             pltpu.VMEM((channels, table), BF16),
@@ -310,10 +339,10 @@
             pltpu.SemaphoreType.DMA((GROUPS * steps,)),
         ],
         compiler_params=pltpu.CompilerParams(
-            collective_id=0, has_side_effects=True, vmem_limit_bytes=48 * 1024 * 1024
+            collective_id=0, has_side_effects=True, vmem_limit_bytes=63 * 1024 * 1024
         ),
         name="sparse_conv",
-    )(features[0], weights, kernel_map[0], send_rows[0], counts, cotangent[0])
+    )(features[0], weights, kernel_map.transpose(1, 0, 2), send_rows[0], counts, cotangent[0])
     return (
         result[None],
         grad_features[None],

time: 61.5 us -> 65 us (1.057)
  Pallas kernels: 52.9 us -> 57.5 us
  local copies, waits for them, and re-layouts: 6.99 us -> 6.01 us
    pallas_call x1, Pallas kernels: 52.9 us -> 57.5 us  [per_device(): pl.pallas_call(functools.partial(kernel, n_space, n_batch, scale), out_sh...]
    unnamed x12 -> x3, local copies, waits for them, and re-layouts: 6.99 us -> 6.01 us
where the time goes in v2:
time: 65 us; the launch traced here: 64.8 us
  Pallas kernels  57.5 us (88%)
  local copies, waits for them, and re-layouts  6.01 us (9%)
  between operations  1.29 us (2%)
    pallas_call x1, Pallas kernels, per_device(): pl.pallas_call(functools.partial(kernel, n_space, n_batch, scale), out_sh...  57.5 us
    unnamed x3, local copies, waits for them, and re-layouts  6.01 us

profile of v2, /device:TPU:0, one launch (start us, length us, event | category | flops | bytes accessed | tf_op | source)
XLA Modules:
  0.0 64.8 jit_solution(10351749124207067728)
XLA Ops:
  1.3 57.5 %sparse_conv.1 = (bf16[512,128]{1,0:T(8,128)(2,1)}, bf16[512,128]{1,0:T(8,128)(2,1)}, f32[27,16,8,128]{3,2,1,0:T(8,128)}) custom-call(bf16[512,128]{1,0:T(8,128)(2,1)} %bitcast.8, bf16[27,128,128]{2,1,0:T(8,128)(2,1)} %w_hbm.1, s32[27,1,512]{2,1,0:T(1,128)} %bitcast.12, s32[2,128]{1,0:T(2,128)} %bitcast.13, s32[1,1]{1,0:T(1,128)S(6)} %copy.12.count, ...), custom_call_target="tpu_custom_call" | custom-call | tf_op jit(solution)/shard_map/sparse_conv/pallas_call | solution.py:307
  58.8 1.6 %copy.13 = bf16[1,512,128]{2,1,0:T(8,128)(2,1)} copy(bf16[1,512,128]{2,1,0:T(8,128)(2,1)} %bitcast.11) | data formatting | bytes 262144
  60.4 1.6 %copy.14 = bf16[1,512,128]{2,1,0:T(8,128)(2,1)} copy(bf16[1,512,128]{2,1,0:T(8,128)(2,1)} %bitcast.10) | data formatting | bytes 262144
  61.9 2.9 %copy.15 = f32[27,128,128]{2,1,0:T(8,128)} copy(f32[27,128,128]{2,1,0:T(8,128)} %bitcast.7) | data formatting | bytes 3538944

commit v3 on v2

--- a/solution.py
+++ b/solution.py
@@ -11,9 +11,11 @@
 BF16 = jnp.bfloat16
 MESH = pl.DeviceIdType.MESH
 BATCH = 3
-SIZES = (4, 3, 2)
+SIZES = (8, 8, 8, 4)
+FIRSTS = (0, 8, 16, 24)
+ROUNDED = 28
 GROUPS = len(SIZES)
-EARLY = 2
+EARLY = 1
 TILES = 16
 ROW = 8
 
@@ -49,13 +51,7 @@
 
 def plan(n_space, n_batch):
     bits = mesh_bits(n_space, n_batch)
-    halvings = min(4, len(bits))
-    orders = []
-    for q in range(GROUPS):
-        rest = bits[1:halvings]
-        turn = q % max(len(rest), 1)
-        orders.append(bits[:1] + rest[turn:] + rest[:turn])
-    return orders, bits[halvings:]
+    return [bits[:1], bits[1:3], bits[3:5]] + [[bit] for bit in bits[5:]]
 
 
 def kernel(
@@ -63,24 +59,36 @@
     feat_hbm, w_hbm, kmap_hbm, send_hbm, count, cot_hbm,
     out, gfeat, gw,
     feat, w, kmap, send, cot, load_sem,
-    ext, outgoing, extt, grad, gt, dw, inbox, acc, gext, back, outt,
+    ext, outgoing, extt, grad, gt, dw, inbox0, inbox1, inbox2, inbox3, acc, gext, back, outt,
     halo_send, halo_recv, back_send, back_recv, sum_send, sum_recv,
 ):
     offsets, channels = w.shape[0], w.shape[1]
     slots = feat.shape[0]
     halo = send.shape[1]
     table = slots + 2 * halo
-    firsts = [BATCH * sum(SIZES[:q]) for q in range(GROUPS)]
     here = {"space": lax.axis_index("space"), "batch": lax.axis_index("batch")}
     s = here["space"]
-    orders, full = plan(n_space, n_batch)
-    halvings = len(orders[0])
+    levels = plan(n_space, n_batch)
 
     def bit_of(bit):
         return (here[bit[0]] // bit[1]) % 2
 
-    def partner(bit):
-        return {**here, bit[0]: here[bit[0]] + bit[1] * (1 - 2 * bit_of(bit))}
+    def member(level, flip=0):
+        place = 0
+        for n, bit in enumerate(levels[level]):
+            value = bit_of(bit)
+            place = place + (1 - value if flip >> n & 1 else value) * (1 << n)
+        return place
+
+    def peer(level, flip):
+        there = dict(here)
+        for n, bit in enumerate(levels[level]):
+            if flip >> n & 1:
+                there[bit[0]] = there[bit[0]] + bit[1] * (1 - 2 * bit_of(bit))
+        return there
+
+    def flips(level):
+        return range(1, 1 << len(levels[level]))
 
     lower = {**here, "space": s - 1}
     upper = {**here, "space": s + 1}
@@ -94,8 +102,11 @@
         loads[name].start()
 
     barrier = pltpu.get_barrier_semaphore()
-    for bit in orders[0] + full:
-        pl.semaphore_signal(barrier, inc=1, device_id=partner(bit), device_id_type=MESH)
+    greeted = 0
+    for level in range(len(levels)):
+        for flip in flips(level):
+            pl.semaphore_signal(barrier, inc=1, device_id=peer(level, flip), device_id_type=MESH)
+            greeted += 1
 
     @pl.when(has_lower)
     def _():
@@ -123,8 +134,8 @@
         ext[slots + halo :] = jnp.zeros((halo, channels), BF16)
         back[:halo] = jnp.zeros((halo, channels), F32)
 
-    neighbours = 1 * (jnp.minimum(s, 1) + jnp.minimum(n_space - 1 - s, 1))
-    pl.semaphore_wait(barrier, len(orders[0] + full) + neighbours)
+    neighbours = jnp.minimum(s, 1) + jnp.minimum(n_space - 1 - s, 1)
+    pl.semaphore_wait(barrier, greeted + neighbours)
 
     to_lower = pltpu.make_async_remote_copy(
         src_ref=outgoing.at[:halo], dst_ref=ext.at[pl.ds(slots + halo, halo)],
@@ -155,58 +166,72 @@
 
     start_both(to_lower, to_upper)
 
-    steps = halvings + len(full) + halvings
+    half, part = TILES // 2, TILES // 8
+    half_at = member(0) * half
+    part_at = half_at + member(1) * part
+    steps = len(levels) + 3
     place = [0] * GROUPS
-    begin = [[0] for _ in range(GROUPS)]
-    flying = [None] * GROUPS
+    flying = [()] * GROUPS
+
+    def offsets_of(q, flip=0):
+        quarter = SIZES[q] // 4
+        return pl.ds(FIRSTS[q] + member(2, flip) * quarter, quarter)
 
     def launch(q):
         step = place[q]
-        ks = pl.ds(firsts[q], BATCH * SIZES[q])
-        sem = q * steps + step
-        if step < halvings:
-            bit = orders[q][step]
-            size = TILES >> (step + 1)
-            src = dw.at[ks, pl.ds(begin[q][-1] + (1 - bit_of(bit)) * size, size)]
-            dst = inbox.at[ks, pl.ds(TILES - 2 * size, size)]
-        elif step < halvings + len(full):
-            bit = full[step - halvings]
-            size = TILES >> halvings
-            src = dw.at[ks, pl.ds(begin[q][-1], size)]
-            dst = inbox.at[ks, pl.ds(TILES - size + (step - halvings) * size, size)]
-        else:
-            level = steps - 1 - step
-            bit = orders[q][level]
-            size = TILES >> (level + 1)
-            src = gw.at[ks, pl.ds(begin[q][level + 1], size)]
-            dst = gw.at[ks, pl.ds(begin[q][level + 1], size)]
-        flying[q] = pltpu.make_async_remote_copy(
-            src_ref=src, dst_ref=dst, send_sem=sum_send.at[sem], recv_sem=sum_recv.at[sem],
-            device_id=partner(bit), device_id_type=MESH)
-        flying[q].start()
+        group = pl.ds(FIRSTS[q], SIZES[q])
+        quarters = pl.ds(FIRSTS[q] // 4, SIZES[q] // 4)
+        level = step if step < len(levels) else steps - 1 - step
+        copies = []
+        for flip in flips(level):
+            if step == 0:
+                src = dw.at[group, pl.ds(member(0, flip) * half, half)]
+                dst = inbox0.at[group]
+            elif step == 1:
+                src = dw.at[group, pl.ds(half_at + member(1, flip) * part, part)]
+                dst = inbox1.at[flip - 1, group]
+            elif step == 2:
+                src = dw.at[offsets_of(q, flip), pl.ds(part_at, part)]
+                dst = inbox2.at[flip - 1, quarters]
+            elif step < len(levels):
+                src = dw.at[offsets_of(q), pl.ds(part_at, part)]
+                dst = inbox3.at[step - 3, quarters]
+            else:
+                tiles = pl.ds(half_at, half) if level == 0 else pl.ds(part_at, part)
+                src = gw.at[offsets_of(q) if level == 2 else group, tiles]
+                dst = src
+            sem = (q * steps + step) * 3 + flip - 1
+            copies.append(pltpu.make_async_remote_copy(
+                src_ref=src, dst_ref=dst, send_sem=sum_send.at[sem], recv_sem=sum_recv.at[sem],
+                device_id=peer(level, flip), device_id_type=MESH))
+            copies[-1].start()
+        flying[q] = copies
 
     def advance(q):
         step = place[q]
         if step >= steps:
             return
-        flying[q].wait()
-        ks = pl.ds(firsts[q], BATCH * SIZES[q])
-        if step < halvings + len(full):
-            if step < halvings:
-                size = TILES >> (step + 1)
-                at = begin[q][-1] + bit_of(orders[q][step]) * size
-                begin[q].append(at)
-                got = pl.ds(TILES - 2 * size, size)
+        for copy in flying[q]:
+            copy.wait()
+        group = pl.ds(FIRSTS[q], SIZES[q])
+        quarters = pl.ds(FIRSTS[q] // 4, SIZES[q] // 4)
+        if step < len(levels):
+            if step == 0:
+                mine = (group, pl.ds(half_at, half))
+                total = dw[mine] + inbox0[group]
+            elif step == 1:
+                mine = (group, pl.ds(part_at, part))
+                total = (dw[mine] + inbox1[0, group]) + (inbox1[1, group] + inbox1[2, group])
             else:
-                size = TILES >> halvings
-                at = begin[q][-1]
-                got = pl.ds(TILES - size + (step - halvings) * size, size)
-            mine = pl.ds(at, size)
-            total = dw[ks, mine] + inbox[ks, got]
-            if step == halvings + len(full) - 1:
-                gw[ks, mine] = total * scale
+                mine = (offsets_of(q), pl.ds(part_at, part))
+                if step == 2:
+                    total = (dw[mine] + inbox2[0, quarters]) + (inbox2[1, quarters] + inbox2[2, quarters])
+                else:
+                    total = dw[mine] + inbox3[step - 3, quarters]
+            if step == len(levels) - 1:
+                gw[mine] = total * scale
             else:
-                dw[ks, mine] = total
+                dw[mine] = total
         place[q] = step + 1
         if place[q] < steps:
             launch(q)
@@ -252,19 +277,24 @@
         return carry
 
     total_loops = offsets // BATCH
-    lax.fori_loop(0, 4, weight_step, 0)
+    dw[offsets:] = jnp.zeros((ROUNDED - offsets, TILES, ROW, channels), F32)
+    lax.fori_loop(0, 3, weight_step, 0)
     launch(0)
-    lax.fori_loop(4, 5, weight_step, 0)
+    lax.fori_loop(3, 4, weight_step, 0)
     advance(0)
-    lax.fori_loop(5, 7, weight_step, 0)
+    lax.fori_loop(4, 6, weight_step, 0)
     launch(1)
-    lax.fori_loop(7, 8, weight_step, 0)
+    lax.fori_loop(6, 7, weight_step, 0)
     advance(0)
     advance(1)
+    lax.fori_loop(7, 8, weight_step, 0)
+    launch(2)
     lax.fori_loop(8, total_loops, weight_step, 0)
-    launch(2)
-    for j in range(EARLY, total_loops):
-        lax.fori_loop(j, j + 1, scatter_step, 0)
+    launch(3)
+    lax.fori_loop(EARLY, 2, scatter_step, 0)
+    advance_all()
+    for j in range(2, total_loops, 2):
+        lax.fori_loop(j, min(j + 2, total_loops), scatter_step, 0)
         advance_all()
 
     both = acc[...]
@@ -277,11 +307,9 @@
         send_sem=back_send.at[1], recv_sem=back_recv.at[1], device_id=upper, device_id_type=MESH)
     start_both(back_lower, back_upper)
 
-    lax.fori_loop(0, 5, forward_step, 0)
+    lax.fori_loop(0, total_loops, forward_step, 0)
     advance_all()
-    lax.fori_loop(5, total_loops, forward_step, 0)
     out[...] = jnp.where(alive, outt[...].T, jnp.zeros((), F32)).astype(BF16)
-    advance_all()
 
     wait_both(back_lower, back_upper)
     lists = jnp.concatenate([send[1:2, :], send[0:1, :]], 1)
@@ -298,8 +326,8 @@
     offsets = weights.shape[0]
     halo = send_rows.shape[2]
     table = slots + 2 * halo
-    orders, full = plan(n_space, n_batch)
-    steps = 2 * len(orders[0]) + len(full)
+    levels = len(plan(n_space, n_batch))
+    steps = levels + 3
     hbm = pl.BlockSpec(memory_space=pltpu.HBM)
     vmem = pl.BlockSpec(memory_space=pltpu.VMEM)
     smem = pl.BlockSpec(memory_space=pltpu.SMEM)
@@ -309,7 +337,7 @@
         out_shape=(
             jax.ShapeDtypeStruct((slots, channels), BF16),
             jax.ShapeDtypeStruct((slots, channels), BF16),
-            jax.ShapeDtypeStruct((offsets, TILES, ROW, channels), F32),
+            jax.ShapeDtypeStruct((ROUNDED, TILES, ROW, channels), F32),
         ),
         in_specs=[hbm, hbm, hbm, hbm, smem, hbm],
         out_specs=(vmem, vmem, vmem),
@@ -325,8 +353,11 @@
             pltpu.VMEM((channels, table), BF16),
             pltpu.VMEM((slots, channels), BF16),
             pltpu.VMEM((offsets * channels, slots), BF16),
-            pltpu.VMEM((offsets, TILES, ROW, channels), F32),
-            pltpu.VMEM((offsets, TILES + len(full), ROW, channels), F32),
+            pltpu.VMEM((ROUNDED, TILES, ROW, channels), F32),
+            pltpu.VMEM((ROUNDED, TILES // 2, ROW, channels), F32),
+            pltpu.VMEM((3, ROUNDED, TILES // 8, ROW, channels), F32),
+            pltpu.VMEM((3, ROUNDED // 4, TILES // 8, ROW, channels), F32),
+            pltpu.VMEM((max(levels - 3, 1), ROUNDED // 4, TILES // 8, ROW, channels), F32),
             pltpu.VMEM((table, 2 * channels), F32),
             pltpu.VMEM((table, channels), F32),
             pltpu.VMEM((2 * halo, channels), F32),
@@ -335,18 +366,18 @@
             pltpu.SemaphoreType.DMA((2,)),
             pltpu.SemaphoreType.DMA((2,)),
             pltpu.SemaphoreType.DMA((2,)),
-            pltpu.SemaphoreType.DMA((GROUPS * steps,)),
-            pltpu.SemaphoreType.DMA((GROUPS * steps,)),
+            pltpu.SemaphoreType.DMA((GROUPS * steps * 3,)),
+            pltpu.SemaphoreType.DMA((GROUPS * steps * 3,)),
         ],
         compiler_params=pltpu.CompilerParams(
-            collective_id=0, has_side_effects=True, vmem_limit_bytes=63 * 1024 * 1024
+            collective_id=0, has_side_effects=True, vmem_limit_bytes=48 * 1024 * 1024
         ),
         name="sparse_conv",
-    )(features[0], weights, kernel_map.transpose(1, 0, 2), send_rows[0], counts, cotangent[0])
+    )(*[pltpu.with_memory_space_constraint(v, pltpu.HBM) for v in (features[0], weights, kernel_map.transpose(1, 0, 2), send_rows[0])], counts, pltpu.with_memory_space_constraint(cotangent[0], pltpu.HBM))
     return (
         result[None],
         grad_features[None],
-        grad_weights.reshape(offsets, channels, channels),
+        grad_weights[:offsets].reshape(offsets, channels, channels),
     )
 
 

time: 65 us -> 53.8 us (0.83)
  Pallas kernels: 57.5 us -> 49.7 us
  local copies, waits for them, and re-layouts: 6.01 us -> 2.71 us
    pallas_call x1, Pallas kernels: 57.5 us -> 49.7 us  [per_device(): pl.pallas_call(functools.partial(kernel, n_space, n_batch, scale), out_sh...]
    unnamed x3 -> x2, local copies, waits for them, and re-layouts: 6.01 us -> 1.31 us
    reshape x0 -> x1, local copies, waits for them, and re-layouts: none -> 1.4 us  [per_device(): grad_weights[:offsets].reshape(offsets, channels, channels)]
where the time goes in v3:
time: 53.8 us; the launch traced here: 53.7 us
  Pallas kernels  49.7 us (92%)
  local copies, waits for them, and re-layouts  2.71 us (5%)
  between operations  1.29 us (2%)
    pallas_call x1, Pallas kernels, per_device(): pl.pallas_call(functools.partial(kernel, n_space, n_batch, scale), out_sh...  49.7 us
    reshape x1, local copies, waits for them, and re-layouts, per_device(): grad_weights[:offsets].reshape(offsets, channels, channels)  1.4 us
    unnamed x2, local copies, waits for them, and re-layouts  1.31 us

profile of v3, /device:TPU:0, one launch (start us, length us, event | category | flops | bytes accessed | tf_op | source)
XLA Modules:
  0.0 53.7 jit_solution(18408926654999640229)
XLA Ops:
  1.3 49.7 %sparse_conv.1 = (bf16[512,128]{1,0:T(8,128)(2,1)S(1)}, bf16[512,128]{1,0:T(8,128)(2,1)S(1)}, f32[28,16,8,128]{3,2,1,0:T(8,128)S(1)}) custom-call(bf16[512,128]{1,0:T(8,128)(2,1)} %bitcast.10, bf16[27,128,128]{2,1,0:T(8,128)(2,1)} %w_hbm.1, s32[27,1,512]{2,1,0:T(1,128)} %bitcast.12, s32[2,128]{1,0:T(2,128)} %bitcast.13, s32[1,1]{1,0:T(1,128)S(6)} %copy.11.count, ...), custom_call_target="tpu_custom_call" | custom-call | tf_op jit(solution)/shard_map/sparse_conv/pallas_call | solution.py:335
  51.0 1.4 %slice_bitcast_fusion = f32[27,128,128]{2,1,0:T(8,128)} fusion(f32[28,16,8,128]{3,2,1,0:T(8,128)S(1)} %get-tuple-element.8), kind=kLoop, calls=%fused_computation | loop fusion | bytes 3538944 | tf_op jit(solution)/shard_map/reshape | solution.py:380
  52.4 0.7 %copy.12 = bf16[1,512,128]{2,1,0:T(8,128)(2,1)} copy(bf16[1,512,128]{2,1,0:T(8,128)(2,1)S(1)} %bitcast.9) | data formatting | bytes 262144
  53.0 0.7 %copy.13 = bf16[1,512,128]{2,1,0:T(8,128)(2,1)} copy(bf16[1,512,128]{2,1,0:T(8,128)(2,1)S(1)} %bitcast.8) | data formatting | bytes 262144

commit v4 on v3

--- a/solution.py
+++ b/solution.py
@@ -171,13 +171,12 @@
     part_at = half_at + member(1) * part
     steps = len(levels) + 3
     place = [0] * GROUPS
-    flying = [()] * GROUPS
 
     def offsets_of(q, flip=0):
         quarter = SIZES[q] // 4
         return pl.ds(FIRSTS[q] + member(2, flip) * quarter, quarter)
 
-    def launch(q):
+    def copies_of(q):
         step = place[q]
         group = pl.ds(FIRSTS[q], SIZES[q])
         quarters = pl.ds(FIRSTS[q] // 4, SIZES[q] // 4)
@@ -204,14 +203,17 @@
             copies.append(pltpu.make_async_remote_copy(
                 src_ref=src, dst_ref=dst, send_sem=sum_send.at[sem], recv_sem=sum_recv.at[sem],
                 device_id=peer(level, flip), device_id_type=MESH))
-            copies[-1].start()
-        flying[q] = copies
+        return copies
+
+    def launch(q):
+        for copy in copies_of(q):
+            copy.start()
 
     def advance(q):
         step = place[q]
         if step >= steps:
             return
-        for copy in flying[q]:
+        for copy in copies_of(q):
             copy.wait()
         group = pl.ds(FIRSTS[q], SIZES[q])
         quarters = pl.ds(FIRSTS[q] // 4, SIZES[q] // 4)
@@ -256,7 +258,7 @@
         acc[...] += dot(jnp.concatenate(picks, 1), jnp.concatenate(parts, 0))
         return carry
 
-    lax.fori_loop(0, EARLY, scatter_step, 0)
+    scatter_step(0, 0)
     wait_both(to_lower, to_upper)
     extt[...] = ext[...].astype(F32).T.astype(BF16)
 
@@ -278,24 +280,47 @@
 
     total_loops = offsets // BATCH
     dw[offsets:] = jnp.zeros((ROUNDED - offsets, TILES, ROW, channels), F32)
-    lax.fori_loop(0, 3, weight_step, 0)
-    launch(0)
-    lax.fori_loop(3, 4, weight_step, 0)
-    advance(0)
-    lax.fori_loop(4, 6, weight_step, 0)
-    launch(1)
-    lax.fori_loop(6, 7, weight_step, 0)
-    advance(0)
-    advance(1)
-    lax.fori_loop(7, 8, weight_step, 0)
-    launch(2)
-    lax.fori_loop(8, total_loops, weight_step, 0)
-    launch(3)
-    lax.fori_loop(EARLY, 2, scatter_step, 0)
-    advance_all()
-    for j in range(2, total_loops, 2):
-        lax.fori_loop(j, min(j + 2, total_loops), scatter_step, 0)
-        advance_all()
+
+    def after_weights(j):
+        @pl.when(j == 2)
+        def _():
+            launch(0)
+
+        @pl.when(j == 3)
+        def _():
+            advance(0)
+
+        @pl.when(j == 5)
+        def _():
+            launch(1)
+
+        @pl.when(j == 6)
+        def _():
+            advance(0)
+            advance(1)
+
+        @pl.when(j == 7)
+        def _():
+            launch(2)
+
+        @pl.when(j == 8)
+        def _():
+            launch(3)
+
+    def weight_stage(j, carry):
+        weight_step(j, carry)
+        after_weights(j)
+        return carry
+
+    def scatter_stage(j, carry):
+        scatter_step(j, carry)
+        forward_step(j, carry)
+        for tick in (1, 3, 4, 6, 8):
+            pl.when(j == tick)(lambda tick=tick: advance_all())
+        return carry
+
+    lax.fori_loop(0, total_loops, weight_stage, 0)
+    lax.fori_loop(EARLY, total_loops, scatter_stage, 0)
 
     both = acc[...]
     gext[...] = both[:, :channels] + both[:, channels:]
@@ -307,8 +332,7 @@
         send_sem=back_send.at[1], recv_sem=back_recv.at[1], device_id=upper, device_id_type=MESH)
     start_both(back_lower, back_upper)
 
-    lax.fori_loop(0, total_loops, forward_step, 0)
-    advance_all()
+    forward_step(0, 0)
     out[...] = jnp.where(alive, outt[...].T, jnp.zeros((), F32)).astype(BF16)
 
     wait_both(back_lower, back_upper)

time: 53.8 us -> 53.9 us (level)
  no operation moved by 1% of the time
where the time goes in v4:
time: 53.9 us; the launch traced here: 53.7 us
  Pallas kernels  49.7 us (92%)
  local copies, waits for them, and re-layouts  2.71 us (5%)
  between operations  1.29 us (2%)
    pallas_call x1, Pallas kernels, per_device(): pl.pallas_call(functools.partial(kernel, n_space, n_batch, scale), out_sh...  49.7 us
    reshape x1, local copies, waits for them, and re-layouts, per_device(): grad_weights[:offsets].reshape(offsets, channels, channels)  1.4 us
    unnamed x2, local copies, waits for them, and re-layouts  1.31 us

profile of v4, /device:TPU:0, one launch (start us, length us, event | category | flops | bytes accessed | tf_op | source)
XLA Modules:
  0.0 53.7 jit_solution(4733829476679168063)
XLA Ops:
  1.3 49.7 %sparse_conv.1 = (bf16[512,128]{1,0:T(8,128)(2,1)S(1)}, bf16[512,128]{1,0:T(8,128)(2,1)S(1)}, f32[28,16,8,128]{3,2,1,0:T(8,128)S(1)}) custom-call(bf16[512,128]{1,0:T(8,128)(2,1)} %bitcast.10, bf16[27,128,128]{2,1,0:T(8,128)(2,1)} %w_hbm.1, s32[27,1,512]{2,1,0:T(1,128)} %bitcast.12, s32[2,128]{1,0:T(2,128)} %bitcast.13, s32[1,1]{1,0:T(1,128)S(6)} %copy.11.count, ...), custom_call_target="tpu_custom_call" | custom-call | tf_op jit(solution)/shard_map/sparse_conv/pallas_call | solution.py:359
  51.0 1.4 %slice_bitcast_fusion = f32[27,128,128]{2,1,0:T(8,128)} fusion(f32[28,16,8,128]{3,2,1,0:T(8,128)S(1)} %get-tuple-element.8), kind=kLoop, calls=%fused_computation | loop fusion | bytes 3538944 | tf_op jit(solution)/shard_map/reshape | solution.py:404
  52.4 0.7 %copy.12 = bf16[1,512,128]{2,1,0:T(8,128)(2,1)} copy(bf16[1,512,128]{2,1,0:T(8,128)(2,1)S(1)} %bitcast.9) | data formatting | bytes 262144
  53.0 0.7 %copy.13 = bf16[1,512,128]{2,1,0:T(8,128)(2,1)} copy(bf16[1,512,128]{2,1,0:T(8,128)(2,1)S(1)} %bitcast.8) | data formatting | bytes 262144

commit v5 on v4

--- a/solution.py
+++ b/solution.py
@@ -263,12 +263,12 @@
     extt[...] = ext[...].astype(F32).T.astype(BF16)
 
     def weight_step(j, carry):
-        for t in range(BATCH):
-            k = j * BATCH + t
-            picked = onehot_columns(kmap[k], table)
-            gathered = dot(extt[...], picked).astype(BF16)
-            gt[pl.ds(pl.multiple_of(k * channels, channels), channels)] = gathered
-            dw[k] = dot(gathered, grad[...]).reshape(TILES, ROW, channels)
+        size = BATCH * channels
+        picks = [onehot_columns(kmap[j * BATCH + t], table) for t in range(BATCH)]
+        gathered = jnp.concatenate([dot(extt[...], picked).astype(BF16) for picked in picks], 0)
+        gt[pl.ds(pl.multiple_of(j * size, size), size)] = gathered
+        products = dot(gathered, grad[...])
+        dw[pl.ds(j * BATCH, BATCH)] = products.reshape(BATCH, TILES, ROW, channels)
         return carry
 
     def forward_step(j, carry):
@@ -312,15 +312,22 @@
         after_weights(j)
         return carry
 
-    def scatter_stage(j, carry):
-        scatter_step(j, carry)
-        forward_step(j, carry)
-        for tick in (1, 3, 4, 6, 8):
-            pl.when(j == tick)(lambda tick=tick: advance_all())
-        return carry
-
+    def scatter_stage(ticks, forward):
+        def stage(j, carry):
+            scatter_step(j, carry)
+            if forward:
+                forward_step(j, carry)
+            for tick in ticks:
+                pl.when(j == tick)(lambda tick=tick: advance_all())
+            return carry
+
+        return stage
+
+    late = 2 * total_loops // 3
     lax.fori_loop(0, total_loops, weight_stage, 0)
-    lax.fori_loop(EARLY, total_loops, scatter_stage, 0)
+    forward_step(0, 0)
+    lax.fori_loop(EARLY, late, scatter_stage((1, 3, 4), True), 0)
+    lax.fori_loop(late, total_loops, scatter_stage((6, 8), False), 0)
 
     both = acc[...]
     gext[...] = both[:, :channels] + both[:, channels:]
@@ -332,7 +339,7 @@
         send_sem=back_send.at[1], recv_sem=back_recv.at[1], device_id=upper, device_id_type=MESH)
     start_both(back_lower, back_upper)
 
-    forward_step(0, 0)
+    lax.fori_loop(late, total_loops, forward_step, 0)
     out[...] = jnp.where(alive, outt[...].T, jnp.zeros((), F32)).astype(BF16)
 
     wait_both(back_lower, back_upper)

time: 53.9 us -> 52.8 us (0.980)
  Pallas kernels: 49.7 us -> 48.7 us
    pallas_call x1, Pallas kernels: 49.7 us -> 48.7 us  [per_device(): pl.pallas_call(functools.partial(kernel, n_space, n_batch, scale), out_sh...]
where the time goes in v5:
time: 52.8 us; the launch traced here: 52.7 us
  Pallas kernels  48.7 us (92%)
  local copies, waits for them, and re-layouts  2.71 us (5%)
  between operations  1.29 us (2%)
    pallas_call x1, Pallas kernels, per_device(): pl.pallas_call(functools.partial(kernel, n_space, n_batch, scale), out_sh...  48.7 us
    reshape x1, local copies, waits for them, and re-layouts, per_device(): grad_weights[:offsets].reshape(offsets, channels, channels)  1.4 us
    unnamed x2, local copies, waits for them, and re-layouts  1.31 us

profile of v5, /device:TPU:0, one launch (start us, length us, event | category | flops | bytes accessed | tf_op | source)
XLA Modules:
  0.0 52.7 jit_solution(6884751637616551500)
XLA Ops:
  1.3 48.7 %sparse_conv.1 = (bf16[512,128]{1,0:T(8,128)(2,1)S(1)}, bf16[512,128]{1,0:T(8,128)(2,1)S(1)}, f32[28,16,8,128]{3,2,1,0:T(8,128)S(1)}) custom-call(bf16[512,128]{1,0:T(8,128)(2,1)} %bitcast.10, bf16[27,128,128]{2,1,0:T(8,128)(2,1)} %w_hbm.1, s32[27,1,512]{2,1,0:T(1,128)} %bitcast.12, s32[2,128]{1,0:T(2,128)} %bitcast.13, s32[1,1]{1,0:T(1,128)S(6)} %copy.11.count, ...), custom_call_target="tpu_custom_call" | custom-call | tf_op jit(solution)/shard_map/sparse_conv/pallas_call | solution.py:366
  49.9 1.4 %slice_bitcast_fusion = f32[27,128,128]{2,1,0:T(8,128)} fusion(f32[28,16,8,128]{3,2,1,0:T(8,128)S(1)} %get-tuple-element.8), kind=kLoop, calls=%fused_computation | loop fusion | bytes 3538944 | tf_op jit(solution)/shard_map/reshape | solution.py:411
  51.3 0.7 %copy.12 = bf16[1,512,128]{2,1,0:T(8,128)(2,1)} copy(bf16[1,512,128]{2,1,0:T(8,128)(2,1)S(1)} %bitcast.9) | data formatting | bytes 262144
  52.0 0.7 %copy.13 = bf16[1,512,128]{2,1,0:T(8,128)(2,1)} copy(bf16[1,512,128]{2,1,0:T(8,128)(2,1)S(1)} %bitcast.8) | data formatting | bytes 262144

commit v6 on v5

--- a/solution.py
+++ b/solution.py
@@ -18,16 +18,21 @@
 EARLY = 1
 TILES = 16
 ROW = 8
+LANES = 128
 
 
 def dot(a, b, contract=((1,), (0,))):
     return lax.dot_general(a, b, (contract, ((), ())), preferred_element_type=F32)
 
 
-def onehot_columns(row, height):
-    line = lax.broadcasted_iota(jnp.int16, (height, row.shape[1]), 0)
-    hit = line == jnp.broadcast_to(row.astype(jnp.int16), line.shape)
-    return jnp.where(hit, jnp.ones((), BF16), jnp.zeros((), BF16))
+def onehot_columns(row, lines):
+    lines = lines[...]
+    row = row.astype(jnp.int16)
+    blocks = []
+    for at in range(0, row.shape[1], LANES):
+        hit = lines == jnp.broadcast_to(row[:, at : at + LANES], lines.shape)
+        blocks.append(jnp.where(hit, jnp.ones((), BF16), jnp.zeros((), BF16)))
+    return jnp.concatenate(blocks, 1)
 
 
 def split_pair(x):
@@ -58,7 +63,7 @@
     n_space, n_batch, scale,
     feat_hbm, w_hbm, kmap_hbm, send_hbm, count, cot_hbm,
     out, gfeat, gw,
-    feat, w, kmap, send, cot, load_sem,
+    feat, w, kmap, send, cot, load_sem, lines,
     ext, outgoing, extt, grad, gt, dw, inbox0, inbox1, inbox2, inbox3, acc, gext, back, outt,
     halo_send, halo_recv, back_send, back_recv, sum_send, sum_recv,
 ):
@@ -101,6 +106,7 @@
         loads[name] = pltpu.make_async_copy(src, dst, load_sem.at[n])
         loads[name].start()
 
+    lines[...] = lax.broadcasted_iota(jnp.int16, lines.shape, 0)
     barrier = pltpu.get_barrier_semaphore()
     greeted = 0
     for level in range(len(levels)):
@@ -122,7 +128,7 @@
     ext[:slots] = live
     loads["send"].wait()
     lists = jnp.concatenate([send[0:1, :], send[1:2, :]], 1)
-    outgoing[...] = dot(onehot_columns(lists, slots), live, ((0,), (0,))).astype(BF16)
+    outgoing[...] = dot(onehot_columns(lists, lines.at[:slots]), live, ((0,), (0,))).astype(BF16)
 
     @pl.when(s == 0)
     def _():
@@ -253,7 +259,7 @@
         contrib = dot(grad[...], weights, ((1,), (1,)))
         picks, parts = [], []
         for t in range(BATCH):
-            picks.append(onehot_columns(kmap[j * BATCH + t], table))
+            picks.append(onehot_columns(kmap[j * BATCH + t], lines))
             parts.append(split_pair(contrib[:, t * channels : (t + 1) * channels]))
         acc[...] += dot(jnp.concatenate(picks, 1), jnp.concatenate(parts, 0))
         return carry
@@ -264,7 +270,7 @@
 
     def weight_step(j, carry):
         size = BATCH * channels
-        picks = [onehot_columns(kmap[j * BATCH + t], table) for t in range(BATCH)]
+        picks = [onehot_columns(kmap[j * BATCH + t], lines) for t in range(BATCH)]
         gathered = jnp.concatenate([dot(extt[...], picked).astype(BF16) for picked in picks], 0)
         gt[pl.ds(pl.multiple_of(j * size, size), size)] = gathered
         products = dot(gathered, grad[...])
@@ -344,7 +350,7 @@
 
     wait_both(back_lower, back_upper)
     lists = jnp.concatenate([send[1:2, :], send[0:1, :]], 1)
-    extra = dot(onehot_columns(lists, slots), split_pair(back[...]))
+    extra = dot(onehot_columns(lists, lines.at[:slots]), split_pair(back[...]))
     local = gext[:slots] + extra[:, :channels] + extra[:, channels:]
     gfeat[...] = jnp.where(alive, local, jnp.zeros((), F32)).astype(BF16)
 
@@ -379,6 +385,7 @@
             pltpu.VMEM((2, halo), jnp.int32),
             pltpu.VMEM((slots, channels), BF16),
             pltpu.SemaphoreType.DMA((5,)),
+            pltpu.VMEM((table, LANES), jnp.int16),
             pltpu.VMEM((table, channels), BF16),
             pltpu.VMEM((2 * halo, channels), BF16),
             pltpu.VMEM((channels, table), BF16),

time: 52.8 us -> 53.4 us (1.011)
    pallas_call x1, Pallas kernels: 48.7 us -> 49.2 us  [per_device(): pl.pallas_call(functools.partial(kernel, n_space, n_batch, scale), out_sh...]
where the time goes in v6:
time: 53.4 us; the launch traced here: 53.2 us
  Pallas kernels  49.2 us (92%)
  local copies, waits for them, and re-layouts  2.71 us (5%)
  between operations  1.29 us (2%)
    pallas_call x1, Pallas kernels, per_device(): pl.pallas_call(functools.partial(kernel, n_space, n_batch, scale), out_sh...  49.2 us
    reshape x1, local copies, waits for them, and re-layouts, per_device(): grad_weights[:offsets].reshape(offsets, channels, channels)  1.4 us
    unnamed x2, local copies, waits for them, and re-layouts  1.31 us

profile of v6, /device:TPU:0, one launch (start us, length us, event | category | flops | bytes accessed | tf_op | source)
XLA Modules:
  0.0 53.2 jit_solution(16145963876663239996)
XLA Ops:
  1.3 49.2 %sparse_conv.1 = (bf16[512,128]{1,0:T(8,128)(2,1)S(1)}, bf16[512,128]{1,0:T(8,128)(2,1)S(1)}, f32[28,16,8,128]{3,2,1,0:T(8,128)S(1)}) custom-call(bf16[512,128]{1,0:T(8,128)(2,1)} %bitcast.10, bf16[27,128,128]{2,1,0:T(8,128)(2,1)} %w_hbm.1, s32[27,1,512]{2,1,0:T(1,128)} %bitcast.12, s32[2,128]{1,0:T(2,128)} %bitcast.13, s32[1,1]{1,0:T(1,128)S(6)} %copy.11.count, ...), custom_call_target="tpu_custom_call" | custom-call | tf_op jit(solution)/shard_map/sparse_conv/pallas_call | solution.py:372
  50.5 1.4 %slice_bitcast_fusion = f32[27,128,128]{2,1,0:T(8,128)} fusion(f32[28,16,8,128]{3,2,1,0:T(8,128)S(1)} %get-tuple-element.8), kind=kLoop, calls=%fused_computation | loop fusion | bytes 3538944 | tf_op jit(solution)/shard_map/reshape | solution.py:418
  51.9 0.7 %copy.12 = bf16[1,512,128]{2,1,0:T(8,128)(2,1)} copy(bf16[1,512,128]{2,1,0:T(8,128)(2,1)S(1)} %bitcast.9) | data formatting | bytes 262144
  52.5 0.7 %copy.13 = bf16[1,512,128]{2,1,0:T(8,128)(2,1)} copy(bf16[1,512,128]{2,1,0:T(8,128)(2,1)S(1)} %bitcast.8) | data formatting | bytes 262144
